TPU v7x, 32 devices: a whole 2x2x4 slice. The times are simulated.
32 devices in a mesh: tm: 16 (over z, y, x), space: 2 (over core).
Axes of the slice: x: 2, y: 2, z: 4, core: 2. Of those that a mesh axis runs over, the one named last changes fastest.
Arguments:
- snapshots: float32 [4096, 3, 1024], P('tm', None, 'space'), may hold values from -108 to 108
- weights: float32 [1024], P('space'), may hold values from 0.1 to 1
- start: float32 [2, 15, 8], replicated, may hold values from -6 to 6
Outputs:
- mode_out: float32 [64, 8, 2, 3, 1024], P('tm', None, None, None, 'space')
- energy: float32 [64, 8], P('tm')
All inputs are finite; a program needn't handle non-finite values.
Results may differ from a plain program's by a relative error of at most 0.0003.
Values sent between devices are 32-bit elements; how exact they have to be, the bound alone decides.
A program may use at most 64 MiB of HBM per device.

v0:
```python
import math
import jax
import jax.numpy as jnp
from jax import lax
from jax.sharding import PartitionSpec as P

NF = 64
ITERS = 8
precise = lax.Precision.HIGHEST
epsilon = 1e-06


def shifted(block, axis, distance):
    devices = range(lax.axis_size(axis))
    route = [(i - distance, i) for i in devices if i - distance in devices]
    return lax.ppermute(block, axis, route)


def dft_table(freqs, seg_len):
    length = 2 * seg_len
    times = jnp.arange(length, dtype=jnp.int32)
    freq_ids = jnp.arange(freqs, dtype=jnp.int32)
    turns = jnp.mod(freq_ids[:, None] * times[None, :], length).astype(jnp.float32)
    phase = 2.0 * math.pi / length * turns
    window = 0.5 - 0.5 * jnp.cos(2.0 * math.pi / length * times.astype(jnp.float32))
    factor = 1.0 / jnp.sqrt(jnp.sum(window * window))
    return jnp.concatenate([window * jnp.cos(phase) * factor, -window * jnp.sin(phase) * factor], 0)


def gram_parts(spectra, col_weights, total_points):
    weighted = spectra * col_weights
    grams = jnp.einsum("nrfc,msfc->frnsm", spectra, weighted, precision=precise)
    gram_re = (grams[:, 0, :, 0, :] + grams[:, 1, :, 1, :]) / total_points
    gram_im = (grams[:, 0, :, 1, :] - grams[:, 1, :, 0, :]) / total_points
    return (gram_re, gram_im)


def apply_gram(gram_re, gram_im, vec_re, vec_im):
    img_re = jnp.einsum("fnm,fmk->fnk", gram_re, vec_re, precision=precise) - jnp.einsum(
        "fnm,fmk->fnk", gram_im, vec_im, precision=precise
    )
    img_im = jnp.einsum("fnm,fmk->fnk", gram_re, vec_im, precision=precise) + jnp.einsum(
        "fnm,fmk->fnk", gram_im, vec_re, precision=precise
    )
    return (img_re, img_im)


def orthonormal(img_re, img_im):
    cols_re = []
    cols_im = []
    for column in range(img_re.shape[-1]):
        part_re = img_re[..., column]
        part_im = img_im[..., column]
        if column > 0:
            prev_re = jnp.stack(cols_re, -1)
            prev_im = jnp.stack(cols_im, -1)
            for repeat in range(2):
                coef_re = jnp.sum(
                    prev_re * part_re[..., None] + prev_im * part_im[..., None], axis=1
                )
                coef_im = jnp.sum(
                    prev_re * part_im[..., None] - prev_im * part_re[..., None], axis=1
                )
                part_re = part_re - jnp.sum(
                    prev_re * coef_re[:, None, :] - prev_im * coef_im[:, None, :], axis=-1
                )
                part_im = part_im - jnp.sum(
                    prev_re * coef_im[:, None, :] + prev_im * coef_re[:, None, :], axis=-1
                )
        inverse = 1.0 / jnp.sqrt(jnp.sum(part_re * part_re + part_im * part_im, axis=1) + epsilon)
        cols_re.append(part_re * inverse[:, None])
        cols_im.append(part_im * inverse[:, None])
    return (jnp.stack(cols_re, -1), jnp.stack(cols_im, -1))


def subspace(gram_re, gram_im, start):
    shape = (gram_re.shape[0], start.shape[1], start.shape[2])
    vec_re = jnp.broadcast_to(start[0], shape)
    vec_im = jnp.broadcast_to(start[1], shape)
    for sweep in range(ITERS):
        img_re, img_im = apply_gram(gram_re, gram_im, vec_re, vec_im)
        vec_re, vec_im = orthonormal(img_re, img_im)
    return (vec_re, vec_im)


def project(spectra, vec_re, vec_im):
    real_rows = spectra[:, 0]
    imag_rows = spectra[:, 1]
    mode_re = jnp.einsum("nfc,fnk->fkc", real_rows, vec_re, precision=precise) - jnp.einsum(
        "nfc,fnk->fkc", imag_rows, vec_im, precision=precise
    )
    mode_im = jnp.einsum("nfc,fnk->fkc", real_rows, vec_im, precision=precise) + jnp.einsum(
        "nfc,fnk->fkc", imag_rows, vec_re, precision=precise
    )
    return (mode_re, mode_im)


def body(snapshots, weights, start):
    seg_len, components, points = snapshots.shape
    columns = components * points
    samples = snapshots.reshape(seg_len, columns)
    basis = dft_table(NF, seg_len)
    tm_count = lax.axis_size("tm")
    blocks = tm_count - 1
    later = shifted(samples, "tm", -1)
    window_rows = jnp.concatenate([samples, later], 0)
    spectrum = jnp.dot(basis, window_rows, precision=precise)
    arrived = lax.all_to_all(
        spectrum.reshape(1, 2, NF, columns), "tm", split_axis=2, concat_axis=0, tiled=True
    )
    spectra = arrived[:blocks]
    col_weights = jnp.tile(weights, components)
    total_points = points * lax.axis_size("space")
    gram_re, gram_im = gram_parts(spectra, col_weights, total_points)
    gram_re, gram_im = lax.psum((gram_re, gram_im), "space")
    vec_re, vec_im = subspace(gram_re, gram_im, start)
    mode_re, mode_im = project(spectra, vec_re, vec_im)
    partial_energy = (
        jnp.sum((mode_re * mode_re + mode_im * mode_im) * col_weights, axis=-1) / total_points
    )
    energy = lax.psum(partial_energy, "space")
    inverse = 1.0 / jnp.sqrt(energy + epsilon)
    mode_out = jnp.stack([mode_re, mode_im], 2) * inverse[:, :, None, None]
    freq_count = mode_out.shape[0]
    return (mode_out.reshape(freq_count, mode_out.shape[1], 2, components, points), energy)


def solution(mesh):
    in_specs = (P("tm", None, "space"), P("space"), P())
    out_specs = (P("tm", None, None, None, "space"), P("tm", None))
    return jax.shard_map(body, mesh=mesh, in_specs=in_specs, out_specs=out_specs, check_vma=False)
```

profile of v0, /device:TPU:0, one launch (start us, length us, event | category | flops | bytes accessed | tf_op | source)
XLA Modules:
  0.0 132.0 jit_solution(17040012056975748923)
XLA Ops:
  0.6 1.9 %copy.460 = f32[256,3,512]{0,2,1:T(8,128)S(1)} copy(f32[256,3,512]{2,0,1:T(8,128)} %param.3) | data formatting | bytes 3145728 | tf_op args[0]
  2.5 1.3 collective-permute-start
  3.8 0.6 multiply_reduce_fusion.1
  5.2 0.5 multiply_multiply_fusion
  5.8 35.9 %collective-permute-done = f32[256,1536]{0,1:T(8,128)S(1)} collective-permute-done((f32[256,1536]{0,1:T(8,128)S(1)}, f32[256,1536]{0,1:T(8,128)S(1)}, u32[]{:S(2)}, u32[]{:S(2)}) %collective-permute-start) | collective-permute-done | bytes 1572896 | tf_op jit(solution)/shard_map/ppermute | solution.py:16
  41.7 3.3 %fusion = f32[128,1536]{1,0:T(8,128)S(1)} fusion(f32[256,1536]{0,1:T(8,128)S(1)} %collective-permute-done, f32[256,1536]{0,1:T(8,128)S(1)} %bitcast.878, f32[64,512]{1,0:T(8,128)S(1)} %get-tuple-element.722, f32[64,512]{1,0:T(8,128)S(1)} %get-tuple-element.723), kind=kOutput, calls=%fused_computation | convolution fusion | flops 1208811520 | bytes 4194304 | tf_op jit(solution)/shard_map/dot_general | solution.py:107
  45.1 1.5 %copy.461 = f32[1,2,64,1536]{3,1,0,2:T(2,128)} copy(f32[1,2,64,1536]{3,2,1,0:T(8,128)S(1)} %bitcast.879) | data formatting | bytes 1572864 | tf_op jit(solution)/shard_map/reshape | solution.py:109
  46.6 7.9 %all-to-all-start = ((f32[1,2,64,1536]{3,1,0,2:T(2,128)}), f32[1,2,64,1536]{3,1,0,2:T(2,128)S(1)}, u32[]{:S(2)}, u32[]{:S(2)}) async-start(f32[1,2,64,1536]{3,1,0,2:T(2,128)} %copy.461), calls=%async_computation | async-start | bytes 1572864 | tf_op jit(solution)/shard_map/all_to_all | solution.py:108
  54.5 18.8 %all-to-all-done = f32[1,2,64,1536]{3,1,0,2:T(2,128)S(1)} async-done(((f32[1,2,64,1536]{3,1,0,2:T(2,128)}), f32[1,2,64,1536]{3,1,0,2:T(2,128)S(1)}, u32[]{:S(2)}, u32[]{:S(2)}) %all-to-all-start) | async-done | bytes 786464 | tf_op jit(solution)/shard_map/all_to_all | solution.py:108
  73.4 0.5 copy.724
  73.9 3.4 %convolution_bitcast_fusion = f32[4,2,15,2,15]{2,4,1,3,0:T(8,128)S(1)} fusion(f32[16,1,2,4,1536]{4,0,2,3,1:T(8,128)S(1)} %bitcast.876, f32[1536]{0:T(1024)S(1)} %mul.8264), kind=kOutput, calls=%fused_computation.6 | convolution fusion | flops 66539520 | bytes 1595456 | tf_op jit(solution)/shard_map/nrfc,msfc->frnsm/dot_general | solution.py:32
  77.3 3.8 %all-reduce = (f32[4,15,15]{1,2,0:T(8,128)S(1)}, f32[4,15,15]{1,2,0:T(8,128)S(1)}) all-reduce(f32[4,15,15]{1,2,0:T(8,128)S(1)} %get-tuple-element.477, f32[4,15,15]{1,2,0:T(8,128)S(1)} %get-tuple-element.476), channel_id=1, replica_groups=mesh['tm'=16,'space'=2] {'space'}, use_global_device_ids=true, to_apply=%region_1.2 | all-reduce | flops 1800 | bytes 14400 | tf_op jit(solution)/shard_map/psum | solution.py:115
  81.9 0.2 add_reduce_fusion.270
  82.1 0.2 add_reduce_fusion.269
  87.6 0.2 add_reduce_fusion.260
  87.7 0.2 add_reduce_fusion.259
  93.2 0.2 add_reduce_fusion.250
  93.4 0.2 add_reduce_fusion.249
  98.9 0.2 add_reduce_fusion.240
  99.1 0.2 add_reduce_fusion.239
  104.7 0.2 add_reduce_fusion.229
  110.4 0.2 add_reduce_fusion.219
  116.2 0.2 add_reduce_fusion.209
  121.9 0.2 add_reduce_fusion.199
  126.6 0.3 fusion.9
  126.9 0.3 fusion.10
  127.2 0.3 convolution_subtract_fusion
  127.6 0.4 multiply_reduce_fusion
  128.0 0.2 copy.688
  128.2 2.5 %psum.23 = f32[4,8]{1,0:T(4,128)S(1)} all-reduce(f32[4,8]{1,0:T(4,128)S(1)} %broadcast_multiply_fusion), channel_id=1, replica_groups=mesh['tm'=16,'space'=2] {'space'}, use_global_device_ids=true, to_apply=%region_484.485 | all-reduce | flops 32 | bytes 256 | tf_op jit(solution)/shard_map/psum | solution.py:121
  130.7 0.2 copy.687
  130.9 1.1 maximum_multiply_fusion
  (587 shorter events, 41.6 us)
Async XLA Ops:
  2.5 39.2 %collective-permute-start = (f32[256,1536]{0,1:T(8,128)S(1)}, f32[256,1536]{0,1:T(8,128)S(1)}, u32[]{:S(2)}, u32[]{:S(2)}) collective-permute-start(f32[256,1536]{0,1:T(8,128)S(1)} %bitcast.877), channel_id=1, source_target_pairs={{2,0},{4,2},{6,4},{8,6},{10,8},{12,10},{14,12},{16,14},{18,16},{20... | collective-permute-start | bytes 4718600 | tf_op jit(solution)/shard_map/ppermute | solution.py:16
  45.1 9.4 %copy-start.2 = (f32[512]{0:T(512)S(1)}, f32[512]{0:T(512)}, u32[]{:S(2)}) copy-start(f32[512]{0:T(512)} %param.4) | copy-start | bytes 6148
  45.1 9.4 %copy-start = (f32[2,15,8]{1,2,0:T(8,128)S(1)}, f32[2,15,8]{1,2,0:T(8,128)}, u32[]{:S(2)}) copy-start(f32[2,15,8]{1,2,0:T(8,128)} %param.5) | copy-start | bytes 2884
  46.6 26.8 %all-to-all-start = ((f32[1,2,64,1536]{3,1,0,2:T(2,128)}), f32[1,2,64,1536]{3,1,0,2:T(2,128)S(1)}, u32[]{:S(2)}, u32[]{:S(2)}) async-start(f32[1,2,64,1536]{3,1,0,2:T(2,128)} %copy.461), calls=%async_computation | async-start | bytes 1572864 | tf_op jit(solution)/shard_map/all_to_all | solution.py:108
  130.7 1.3 %copy-start.1 = (f32[4,8]{1,0:T(4,128)}, f32[4,8]{1,0:T(4,128)S(1)}, u32[]{:S(2)}) copy-start(f32[4,8]{1,0:T(4,128)S(1)} %psum.23) | copy-start | bytes 388
where the time goes:
time: 132 us
  waiting for transfers between devices  54.8 us (42%)
  other arithmetic  38.5 us (29%)
  matrix products  13.4 us (10%)
  starting transfers between devices  9.18 us (7%)
  local copies, waits for them, and re-layouts  6.57 us (5%)
  blocking collectives  6.25 us (5%)
  between operations  3.29 us (2%)
    ppermute x1, waiting for transfers between devices, shifted(): return lax.ppermute(block, axis, route)  35.9 us
    all_to_all x1, waiting for transfers between devices, body(): lax.all_to_all(spectrum.reshape(1, 2, NF, columns), 'tm', split_axis=2, c...  18.8 us
    reduce_sum x112, other arithmetic, orthonormal(): jnp.sum(prev_re * part_re[..., None] + prev_im * part_im[..., None], axis=1)  13 us
    reduce_sum x96, other arithmetic, orthonormal(): jnp.sum(prev_re * coef_re[:, None, :] - prev_im * coef_im[:, None, :], ax...  9.33 us
    reduce_sum x64, other arithmetic, orthonormal(): jnp.sum(part_re * part_re + part_im * part_im, axis=1) + epsilon  8.27 us
    all_to_all x1, starting transfers between devices, body(): lax.all_to_all(spectrum.reshape(1, 2, NF, columns), 'tm', split_axis=2, c...  7.89 us
    mul x56, other arithmetic, orthonormal(): cols_re.append(part_re * inverse[:, None])  4.27 us
    psum x1, blocking collectives, body(): gram_re, gram_im = lax.psum((gram_re, gram_im), 'space')  3.78 us
  transfers between devices with their start and end apart: 2, of which 2 were waited for; matrix products, arithmetic and copies ran while one was open for 1% of the time, Pallas kernels for 0%

commit v1 on v0

--- a/solution.py
+++ b/solution.py
@@ -8,6 +8,12 @@
 ITERS = 8
 precise = lax.Precision.HIGHEST
 epsilon = 1e-06
+
+
+def swap_blocks(x, axis, split, join):
+    shards = jnp.split(x, lax.axis_size(axis), axis=split)
+    received = lax.all_to_all(jnp.stack(shards), axis, 0, 0)
+    return jnp.concatenate(received, axis=join)
 
 
 def shifted(block, axis, distance):
@@ -105,9 +111,7 @@
     later = shifted(samples, "tm", -1)
     window_rows = jnp.concatenate([samples, later], 0)
     spectrum = jnp.dot(basis, window_rows, precision=precise)
-    arrived = lax.all_to_all(
-        spectrum.reshape(1, 2, NF, columns), "tm", split_axis=2, concat_axis=0, tiled=True
-    )
+    arrived = swap_blocks(spectrum.reshape(1, 2, NF, columns), "tm", 2, 0)
     spectra = arrived[:blocks]
     col_weights = jnp.tile(weights, components)
     total_points = points * lax.axis_size("space")

time: 132 us -> 142 us (1.076)
  local copies, waits for them, and re-layouts: 6.57 us -> 15.4 us
    unnamed x7 -> x23, local copies, waits for them, and re-layouts: 1.89 us -> 11.9 us
    reshape x1 -> x0, local copies, waits for them, and re-layouts: 1.48 us -> none  [body(): spectrum.reshape(1, 2, NF, columns)]
where the time goes in v1:
time: 142 us; the launch traced here: 141 us
  waiting for transfers between devices  54.8 us (39%)
  other arithmetic  38.5 us (27%)
  local copies, waits for them, and re-layouts  15.4 us (11%)
  matrix products  13.8 us (10%)
  starting transfers between devices  9.18 us (6%)
  blocking collectives  6.25 us (4%)
  between operations  3.3 us (2%)
    ppermute x1, waiting for transfers between devices, shifted(): return lax.ppermute(block, axis, route)  35.9 us
    all_to_all x1, waiting for transfers between devices, swap_blocks(): received = lax.all_to_all(jnp.stack(shards), axis, 0, 0)  18.8 us
    reduce_sum x112, other arithmetic, orthonormal(): jnp.sum(prev_re * part_re[..., None] + prev_im * part_im[..., None], axis=1)  13 us
    unnamed x23, local copies, waits for them, and re-layouts  11.9 us
    reduce_sum x96, other arithmetic, orthonormal(): jnp.sum(prev_re * coef_re[:, None, :] - prev_im * coef_im[:, None, :], ax...  9.33 us
    reduce_sum x64, other arithmetic, orthonormal(): jnp.sum(part_re * part_re + part_im * part_im, axis=1) + epsilon  8.27 us
    all_to_all x1, starting transfers between devices, swap_blocks(): received = lax.all_to_all(jnp.stack(shards), axis, 0, 0)  7.89 us
    mul x56, other arithmetic, orthonormal(): cols_re.append(part_re * inverse[:, None])  4.27 us
  transfers between devices with their start and end apart: 2, of which 2 were waited for; matrix products, arithmetic and copies ran while one was open for 1% of the time, Pallas kernels for 0%

profile of v1, /device:TPU:0, one launch (start us, length us, event | category | flops | bytes accessed | tf_op | source)
XLA Modules:
  0.0 141.3 jit_solution(1799427774813178125)
XLA Ops:
  0.6 1.9 %copy.490 = f32[256,3,512]{0,2,1:T(8,128)S(1)} copy(f32[256,3,512]{2,0,1:T(8,128)} %param.3) | data formatting | bytes 3145728 | tf_op args[0]
  2.5 1.3 collective-permute-start
  3.8 0.6 multiply_reduce_fusion.1
  5.2 0.5 multiply_multiply_fusion
  5.8 35.9 %collective-permute-done = f32[256,1536]{0,1:T(8,128)S(1)} collective-permute-done((f32[256,1536]{0,1:T(8,128)S(1)}, f32[256,1536]{0,1:T(8,128)S(1)}, u32[]{:S(2)}, u32[]{:S(2)}) %collective-permute-start) | collective-permute-done | bytes 1572896 | tf_op jit(solution)/shard_map/ppermute | solution.py:22
  41.7 3.3 %fusion = f32[128,1536]{1,0:T(8,128)S(1)} fusion(f32[256,1536]{0,1:T(8,128)S(1)} %collective-permute-done, f32[256,1536]{0,1:T(8,128)S(1)} %bitcast.941, f32[64,512]{1,0:T(8,128)S(1)} %get-tuple-element.738, f32[64,512]{1,0:T(8,128)S(1)} %get-tuple-element.739), kind=kOutput, calls=%fused_computation | convolution fusion | flops 1208811520 | bytes 4194304 | tf_op jit(solution)/shard_map/dot_general | solution.py:113
  45.2 0.6 fusion.35
  45.9 0.6 fusion.34
  46.5 0.6 fusion.33
  47.2 0.6 fusion.32
  47.8 0.6 fusion.31
  48.4 0.6 fusion.30
  49.1 0.6 fusion.29
  49.7 0.6 fusion.28
  50.4 0.6 fusion.27
  51.0 0.6 fusion.26
  51.6 0.6 fusion.25
  52.3 0.6 fusion.24
  52.9 0.6 fusion.23
  53.6 0.6 fusion.22
  54.2 0.6 fusion.21
  54.8 0.6 fusion.20
  55.5 7.9 %all-to-all-start = ((f32[16,1,2,4,1536]{4,2,3,1,0:T(2,128)}), f32[16,1,2,4,1536]{4,2,3,1,0:T(2,128)S(1)}, u32[]{:S(2)}, u32[]{:S(2)}) async-start(f32[16,1,2,4,1536]{4,2,3,1,0:T(2,128)} %fusion.20), calls=%async_computation | async-start | bytes 1572864 | tf_op jit(solution)/shard_map/all_to_all | solution.py:15
  63.4 18.8 %all-to-all-done = f32[16,1,2,4,1536]{4,2,3,1,0:T(2,128)S(1)} async-done(((f32[16,1,2,4,1536]{4,2,3,1,0:T(2,128)}), f32[16,1,2,4,1536]{4,2,3,1,0:T(2,128)S(1)}, u32[]{:S(2)}, u32[]{:S(2)}) %all-to-all-start) | async-done | bytes 786464 | tf_op jit(solution)/shard_map/all_to_all | solution.py:15
  82.3 0.4 copy.841
  82.8 3.8 %convolution_bitcast_fusion = f32[4,2,15,2,15]{2,4,1,3,0:T(8,128)S(1)} fusion(f32[15,1,2,4,1536]{4,2,3,1,0:T(2,128)S(1)} %slice.552, f32[1536]{0:T(1024)S(1)} %mul.8264), kind=kOutput, calls=%fused_computation.6 | convolution fusion | flops 66539520 | bytes 757824 | tf_op jit(solution)/shard_map/nrfc,msfc->frnsm/dot_general | solution.py:38
  86.5 3.8 %all-reduce = (f32[4,15,15]{1,2,0:T(8,128)S(1)}, f32[4,15,15]{1,2,0:T(8,128)S(1)}) all-reduce(f32[4,15,15]{1,2,0:T(8,128)S(1)} %get-tuple-element.493, f32[4,15,15]{1,2,0:T(8,128)S(1)} %get-tuple-element.492), channel_id=1, replica_groups=mesh['tm'=16,'space'=2] {'space'}, use_global_device_ids=true, to_apply=%region_1.2 | all-reduce | flops 1800 | bytes 14400 | tf_op jit(solution)/shard_map/psum | solution.py:119
  136.1 0.3 fusion.10
  136.5 0.3 convolution_subtract_fusion
  136.8 0.4 multiply_reduce_fusion
  137.5 2.5 %psum.23 = f32[4,8]{1,0:T(4,128)S(1)} all-reduce(f32[4,8]{1,0:T(4,128)S(1)} %broadcast_multiply_fusion), channel_id=1, replica_groups=mesh['tm'=16,'space'=2] {'space'}, use_global_device_ids=true, to_apply=%region_484.485 | all-reduce | flops 32 | bytes 256 | tf_op jit(solution)/shard_map/psum | solution.py:125
  140.2 1.1 maximum_multiply_fusion
  (603 shorter events, 44.8 us)
Async XLA Ops:
  2.5 39.2 %collective-permute-start = (f32[256,1536]{0,1:T(8,128)S(1)}, f32[256,1536]{0,1:T(8,128)S(1)}, u32[]{:S(2)}, u32[]{:S(2)}) collective-permute-start(f32[256,1536]{0,1:T(8,128)S(1)} %bitcast.940), channel_id=1, source_target_pairs={{2,0},{4,2},{6,4},{8,6},{10,8},{12,10},{14,12},{16,14},{18,16},{20... | collective-permute-start | bytes 4718600 | tf_op jit(solution)/shard_map/ppermute | solution.py:22
  45.2 18.2 %copy-start.2 = (f32[512]{0:T(512)S(1)}, f32[512]{0:T(512)}, u32[]{:S(2)}) copy-start(f32[512]{0:T(512)} %param.4) | copy-start | bytes 6148
  45.9 17.5 %copy-start = (f32[2,15,8]{1,2,0:T(8,128)S(1)}, f32[2,15,8]{1,2,0:T(8,128)}, u32[]{:S(2)}) copy-start(f32[2,15,8]{1,2,0:T(8,128)} %param.5) | copy-start | bytes 2884
  55.5 26.8 %all-to-all-start = ((f32[16,1,2,4,1536]{4,2,3,1,0:T(2,128)}), f32[16,1,2,4,1536]{4,2,3,1,0:T(2,128)S(1)}, u32[]{:S(2)}, u32[]{:S(2)}) async-start(f32[16,1,2,4,1536]{4,2,3,1,0:T(2,128)} %fusion.20), calls=%async_computation | async-start | bytes 1572864 | tf_op jit(solution)/shard_map/all_to_all | solution.py:15
  139.9 1.3 copy-start.1
